TPU v7x, 512 devices: a whole 4x8x8 slice. The times are simulated.
512 devices in a mesh: leaf: 128 (over y, z, core), cols: 4 (over x).
Axes of the slice: x: 4, y: 8, z: 8, core: 2. Of those that a mesh axis runs over, the one named last changes fastest.
Arguments:
- samples: bfloat16 [262144, 256], P(('leaf', 'cols')), may hold values from -6 to 6
- near_tiles: bfloat16 [2048, 16, 128, 128], P('leaf', 'cols'), may hold values from -0.1875 to 0.1875
- columns: int32 [2048, 16], P('leaf', 'cols'), may hold values from 0 to 2047, as said below
- tile_count: int32 [2048], P('leaf'), may hold values from 4 to 16, as said below
- skeleton_one: int32 [16, 64, 128], P('cols'), may hold values from 0 to 255, as said below
- skeleton_two: int32 [16, 32, 128], P('cols'), may hold values from 0 to 255, as said below
- skeleton_three: int32 [16, 16, 128], P('cols'), may hold values from 0 to 255, as said below
Outputs:
- transfer_one: float32 [128, 8, 256, 128], P('leaf', 'cols')
- transfer_two: float32 [128, 4, 256, 128], P('leaf', 'cols')
- transfer_three: float32 [128, 4, 256, 128], P('leaf', 'cols')
- top_samples: float32 [128, 4, 128, 256], P('leaf', 'cols')
Inputs may be any that keep to these rules, and one draw needn't show every extreme that they name: `columns`: the column cluster of a slot of row cluster r, of any layer, lies in region r // 16 or a region beside it. `tile_count`: slots at or past a cluster's count are unused; some cluster uses all 16. `skeleton_one`: each row holds 128 distinct indices. `skeleton_two`: each row holds 128 distinct indices. `skeleton_three`: each row holds 128 distinct indices.
All inputs are finite; a program needn't handle non-finite values.
Results may differ from a plain program's by a relative error of at most 0.0003.
Values may be sent and summed in bfloat16 or wider, within the bound.
No kernel may reach another device: no remote copies, remote signals or barrier semaphores. Data moves between devices by JAX's collectives and lax.ppermute only.
A program may use at most 64 MiB of HBM per device.

v0:
```python
import jax
import jax.numpy as jnp
from jax import lax
from jax.sharding import PartitionSpec as P

HIGHEST = lax.Precision.HIGHEST
RIDGE = 0.25


def padded(value, sides, width):
    for axis, dim in sides:
        count, length = (lax.axis_size(axis), value.shape[dim])
        up = [(i, (i + 1) % count) for i in range(count - 1)]
        down = [(j, i) for i, j in up]
        last = lax.slice_in_dim(value, length - width, length, axis=dim)
        initial = lax.slice_in_dim(value, 0, width, axis=dim)
        before = lax.ppermute(last, axis, up)
        after = lax.ppermute(initial, axis, down)
        value = jnp.concatenate([before, value, after], axis=dim)
    return value


def swapped(block, axis, apart):
    count = lax.axis_size(axis)
    route = []
    for low in range(count):
        high = low | 1 << apart
        if high != low and high < count:
            route += [(low, high), (high, low)]
    return lax.ppermute(block, axis, route)


def merge_pair(first, second, chosen):
    stacked = jnp.concatenate([first, second], axis=1)
    picked = jax.vmap(lambda block, index: block[index])(stacked, chosen)
    count = stacked.shape[2]
    rank = picked.shape[1]
    gram = jnp.einsum("mis,mjs->mij", picked, picked, precision=HIGHEST) / count
    gram = gram + RIDGE * jnp.eye(rank, dtype=jnp.float32)
    lower = jnp.linalg.cholesky(gram)
    basis = jax.vmap(
        lambda factor, rhs: jax.scipy.linalg.solve_triangular(factor, rhs, lower=True)
    )(lower, picked)
    transfer = jnp.einsum("mis,mjs->mij", stacked, basis, precision=HIGHEST) / count
    return (basis, transfer)


def local(samples, near_tiles, columns, tile_count, skeleton_one, skeleton_two, skeleton_three):
    leaf_index = lax.axis_index("leaf")
    cols_index = lax.axis_index("cols")
    clusters, slots, panels, _ = near_tiles.shape
    width = samples.shape[1]
    own_rows = lax.all_gather(samples, "cols", axis=0, tiled=True)
    near_rows = padded(own_rows, (("leaf", 0),), own_rows.shape[0])
    window = near_rows.reshape(3 * clusters, panels, width)
    local_cols = columns - (leaf_index - 1) * clusters
    picked = jnp.take(window, local_cols, axis=0)
    slot_ids = cols_index * slots + lax.iota(jnp.int32, slots)
    active = (slot_ids[None, :] < tile_count[:, None]).astype(picked.dtype)
    picked = picked * active[:, :, None, None]
    partial_value = jnp.einsum(
        "ksij,ksjn->kin", near_tiles, picked, preferred_element_type=jnp.float32
    )
    nodes = lax.psum_scatter(partial_value, "cols", scatter_dimension=0, tiled=True)
    subtrees = nodes.shape[0]
    outputs = []
    level = 0
    spread = 1
    for skeleton in (skeleton_one, skeleton_two, skeleton_three):
        level = level + 1
        side = leaf_index >> level - 1 & 1
        group = leaf_index >> level
        spread = min(2**level, subtrees)
        offset = leaf_index % spread
        chosen_all = lax.dynamic_index_in_dim(skeleton, group, axis=1, keepdims=False)
        other = swapped(nodes, "leaf", level - 1)
        first = jnp.where(side == 0, nodes, other)
        second = jnp.where(side == 0, other, nodes)
        basis, transfer = merge_pair(first, second, chosen_all)
        kept = lax.dynamic_index_in_dim(
            transfer.reshape(subtrees // spread, spread, 2 * panels, panels),
            offset,
            axis=1,
            keepdims=False,
        )
        outputs.append(kept[None])
        nodes = basis
    offset = leaf_index % spread
    top = lax.dynamic_index_in_dim(
        nodes.reshape(subtrees // spread, spread, panels, width), offset, axis=1, keepdims=False
    )
    return (outputs[0], outputs[1], outputs[2], top[None])


def solution(mesh):
    placed = (
        P(("leaf", "cols"), None),
        P("leaf", "cols", None, None),
        P("leaf", "cols"),
        P("leaf"),
        P("cols", None, None),
        P("cols", None, None),
        P("cols", None, None),
    )
    return jax.shard_map(
        local,
        mesh=mesh,
        in_specs=placed,
        out_specs=(
            P("leaf", "cols", None, None),
            P("leaf", "cols", None, None),
            P("leaf", "cols", None, None),
            P("leaf", "cols", None, None),
        ),
        check_vma=False,
    )
```

profile of v0, /device:TPU:8, one launch (start us, length us, event | category | flops | bytes accessed | tf_op | source)
XLA Modules:
  0.0 481.1 jit_solution(7024307054163040325)
XLA Ops:
  8.0 36.0 %all-gather.2.cloned.1.call-done = bf16[2048,256]{1,0:T(8,128)(2,1)} async-done(((bf16[512,256]{1,0:T(8,128)(2,1)}), bf16[2048,256]{1,0:T(8,128)(2,1)}) %all-gather.2.cloned.1.call-update) | async-done | bytes 1048592 | tf_op jit(solution)/shard_map/all_gather | solution.py:53
  45.9 5.8 %collective-permute-start.1 = (bf16[2048,256]{1,0:T(8,128)(2,1)}, bf16[2048,256]{1,0:T(8,128)(2,1)}, u32[]{:S(2)}, u32[]{:S(2)}) collective-permute-start(bf16[2048,256]{1,0:T(8,128)(2,1)} %all-gather.2.cloned.1.call-done), channel_id=1, source_target_pairs={{4,0},{8,4},{12,8},{16,12},{20,16},{24,20},{28,24},{32,28},{36,32}... | collective-permute-start | bytes 3145736 | tf_op jit(solution)/shard_map/ppermute | solution.py:18
  53.4 9.0 %collective-permute-done = bf16[2048,256]{1,0:T(8,128)(2,1)S(1)} collective-permute-done((bf16[2048,256]{1,0:T(8,128)(2,1)}, bf16[2048,256]{1,0:T(8,128)(2,1)S(1)}, u32[]{:S(2)}, u32[]{:S(2)}) %collective-permute-start) | collective-permute-done | bytes 1048608 | tf_op jit(solution)/shard_map/ppermute | solution.py:17
  64.3 3.0 pad_maximum_fusion
  67.3 4.6 gather_fusion
  71.9 6.4 %copy.41 = bf16[64,128,256]{1,2,0:T(8,128)(2,1)} copy(bf16[64,128,256]{2,1,0:T(8,128)(2,1)} %gather_fusion) | data formatting | bytes 8388608 | tf_op jit(solution)/shard_map/jit(_take)/gather | solution.py:57
  78.3 4.8 %fusion.6 = f32[16,128,256]{1,2,0:T(8,128)} fusion(bf16[16,4,128,128]{3,2,1,0:T(8,128)(2,1)S(1)} %copy-done, bf16[16,4,128,256]{2,3,1,0:T(8,128)(2,1)} %bitcast.75, pred[16,4]{1,0:T(8,128)(4,1)S(1)} %copy.39, bf16[16,4]{1,0:T(8,128)(2,1)S(1)} %compare_convert_fusion), kind=kOutput, calls=%fused_computation.11 | convolution fusion | flops 541065216 | bytes 8388800 | tf_op jit(solution)/shard_map/ksij,ksjn->kin/dot_general | solution.py:61
  84.0 34.4 %reduce-scatter.2.cloned.1.call-done = f32[4,128,256]{1,2,0:T(8,128)} async-done(((f32[16,128,256]{1,2,0:T(8,128)}), f32[4,128,256]{1,2,0:T(8,128)}) %reduce-scatter.2.cloned.1.call-update) | async-done | bytes 524304 | tf_op jit(solution)/shard_map/reduce_scatter | solution.py:64
  127.0 6.3 %gather_fusion.1 = f32[512,256]{1,0:T(8,128)} fusion(f32[4,256,256]{2,1,0:T(8,128)S(1)} %copy.42, s32[512]{0:T(512)S(1)} %get-tuple-element.14), kind=kCustom, calls=%fused_computation.1 | custom fusion | bytes 1052672 | tf_op jit(solution)/shard_map/vmap()/gather | solution.py:35
  135.4 46.9 %custom-call.16 = f32[4,128,128]{2,1,0:T(8,128)S(1)} custom-call(f32[4,128,128]{2,1,0:T(8,128)S(1)} %fusion.20), custom_call_target="Cholesky" | custom-call | tf_op jit(solution)/shard_map/jit(cholesky)/cholesky | solution.py:40
  182.6 39.3 %custom-call.17 = f32[4,1,128,128]{2,3,1,0:T(8,128)S(1)} custom-call(f32[4,1,128,128]{3,2,1,0:T(8,128)S(1)} %select_bitcast_fusion.2), custom_call_target="InvertDiagBlocksLowerTriangular" | custom-call | tf_op jit(solution)/shard_map/vmap(jit(_solve_triangular))/triangular_solve | solution.py:42
  223.6 3.8 collective-permute-start.3
  228.1 11.3 %collective-permute-done.3 = f32[4,128,256]{2,1,0:T(8,128)S(1)} collective-permute-done((f32[4,128,256]{2,1,0:T(8,128)S(1)}, f32[4,128,256]{2,1,0:T(8,128)S(1)}, u32[]{:S(2)}, u32[]{:S(2)}) %collective-permute-start.3) | collective-permute-done | bytes 524320 | tf_op jit(solution)/shard_map/ppermute | solution.py:30
  240.5 6.4 %gather_fusion.2 = f32[512,256]{1,0:T(8,128)} fusion(f32[4,256,256]{2,1,0:T(8,128)S(1)} %pad_maximum_fusion.2, s32[512]{0:T(512)S(1)} %get-tuple-element.15), kind=kCustom, calls=%fused_computation.2 | custom fusion | bytes 1052672 | tf_op jit(solution)/shard_map/vmap()/gather | solution.py:35
  246.9 1.9 fusion.10
  251.3 47.7 %custom-call.18 = f32[4,128,128]{2,1,0:T(8,128)S(1)} custom-call(f32[4,128,128]{2,1,0:T(8,128)} %fusion.17), custom_call_target="Cholesky" | custom-call | tf_op jit(solution)/shard_map/jit(cholesky)/cholesky | solution.py:40
  300.0 40.1 %custom-call.19 = f32[4,1,128,128]{2,3,1,0:T(8,128)S(1)} custom-call(f32[4,1,128,128]{3,2,1,0:T(8,128)} %select_bitcast_fusion.1), custom_call_target="InvertDiagBlocksLowerTriangular" | custom-call | tf_op jit(solution)/shard_map/vmap(jit(_solve_triangular))/triangular_solve | solution.py:42
  341.9 4.7 collective-permute-start.4
  346.6 2.9 convolution_multiply_fusion
  352.0 17.2 %collective-permute-done.4 = f32[4,128,256]{2,1,0:T(8,128)S(1)} collective-permute-done((f32[4,128,256]{2,1,0:T(8,128)S(1)}, f32[4,128,256]{2,1,0:T(8,128)S(1)}, u32[]{:S(2)}, u32[]{:S(2)}) %collective-permute-start.4) | collective-permute-done | bytes 524320 | tf_op jit(solution)/shard_map/ppermute | solution.py:30
  370.4 6.6 %gather_fusion.3 = f32[512,256]{1,0:T(8,128)} fusion(f32[4,256,256]{2,1,0:T(8,128)S(1)} %pad_maximum_fusion.3, s32[512]{0:T(512)S(1)} %fusion.35), kind=kCustom, calls=%fused_computation.3 | custom fusion | bytes 1052672 | tf_op jit(solution)/shard_map/vmap()/gather | solution.py:35
  377.0 1.9 fusion.11
  381.4 47.7 %custom-call.20 = f32[4,128,128]{2,1,0:T(8,128)S(1)} custom-call(f32[4,128,128]{2,1,0:T(8,128)} %fusion.14), custom_call_target="Cholesky" | custom-call | tf_op jit(solution)/shard_map/jit(cholesky)/cholesky | solution.py:40
  430.0 40.1 %custom-call.21 = f32[4,1,128,128]{2,3,1,0:T(8,128)S(1)} custom-call(f32[4,1,128,128]{3,2,1,0:T(8,128)} %select_bitcast_fusion), custom_call_target="InvertDiagBlocksLowerTriangular" | custom-call | tf_op jit(solution)/shard_map/vmap(jit(_solve_triangular))/triangular_solve | solution.py:42
  (83 shorter events, 37.8 us)
Async XLA Ops:
  7.2 71.2 %copy-start = (bf16[16,4,128,128]{3,2,1,0:T(8,128)(2,1)S(1)}, bf16[16,4,128,128]{3,2,1,0:T(8,128)(2,1)}, u32[]{:S(2)}) copy-start(bf16[16,4,128,128]{3,2,1,0:T(8,128)(2,1)} %param.11) | copy-start | bytes 6291460
  7.2 36.8 %all-gather.2.cloned.1.call-start = ((), (), s32[]{:S(2)}) async-start(), calls=%async_computation.1 | async-start | bytes 1310720 | tf_op jit(solution)/shard_map/all_gather | solution.py:53
  7.9 110.4 %reduce-scatter.2.cloned.1.call-start = ((), (), s32[]{:S(2)}) async-start(), calls=%async_computation.2 | async-start | bytes 2621440 | tf_op jit(solution)/shard_map/reduce_scatter | solution.py:64
  44.0 18.4 %collective-permute-start = (bf16[2048,256]{1,0:T(8,128)(2,1)}, bf16[2048,256]{1,0:T(8,128)(2,1)S(1)}, u32[]{:S(2)}, u32[]{:S(2)}) collective-permute-start(bf16[2048,256]{1,0:T(8,128)(2,1)} %all-gather.2.cloned.1.call-done), channel_id=1, source_target_pairs={{0,4},{4,8},{8,12},{12,16},{16,20},{20,24},{24,28},{28,32},{32,36}... | collective-permute-start | bytes 3145736 | tf_op jit(solution)/shard_map/ppermute | solution.py:17
  45.9 18.4 %collective-permute-start.1 = (bf16[2048,256]{1,0:T(8,128)(2,1)}, bf16[2048,256]{1,0:T(8,128)(2,1)}, u32[]{:S(2)}, u32[]{:S(2)}) collective-permute-start(bf16[2048,256]{1,0:T(8,128)(2,1)} %all-gather.2.cloned.1.call-done), channel_id=1, source_target_pairs={{4,0},{8,4},{12,8},{16,12},{20,16},{24,20},{28,24},{32,28},{36,32}... | collective-permute-start | bytes 3145736 | tf_op jit(solution)/shard_map/ppermute | solution.py:18
  118.3 4.0 collective-permute-start.2
  123.4 0.8 copy-start.3
  123.4 1.0 copy-start.5
  223.6 16.0 %copy-start.1 = (f32[4,128,256]{2,1,0:T(8,128)}, f32[4,128,256]{2,1,0:T(8,128)S(1)}, u32[]{:S(2)}) copy-start(f32[4,128,256]{2,1,0:T(8,128)S(1)} %fusion.18) | copy-start | bytes 1572868
  223.6 15.9 %collective-permute-start.3 = (f32[4,128,256]{2,1,0:T(8,128)S(1)}, f32[4,128,256]{2,1,0:T(8,128)S(1)}, u32[]{:S(2)}, u32[]{:S(2)}) collective-permute-start(f32[4,128,256]{2,1,0:T(8,128)S(1)} %fusion.18), channel_id=1, source_target_pairs={{0,8},{8,0},{4,12},{12,4},{16,24},{24,16},{20,28},{28,20},{32,40},... | collective-permute-start | bytes 1572872 | tf_op jit(solution)/shard_map/ppermute | solution.py:30
  239.6 0.8 copy-start.6
  239.6 1.0 copy-start.8
  246.9 99.7 %copy-start.2 = (f32[4,128,256]{2,1,0:T(8,128)S(1)}, f32[4,128,256]{2,1,0:T(8,128)}, u32[]{:S(2)}) copy-start(f32[4,128,256]{2,1,0:T(8,128)} %copy-done.1) | copy-start | bytes 1572868
  246.9 99.7 %copy-start.4 = (f32[4,128,256]{1,2,0:T(8,128)S(1)}, f32[4,128,256]{1,2,0:T(8,128)}, u32[]{:S(2)}) copy-start(f32[4,128,256]{1,2,0:T(8,128)} %copy-done.3) | copy-start | bytes 1572868
  340.1 10.1 %copy-start.7 = (f32[4,128,256]{2,1,0:T(8,128)S(1)}, f32[4,128,256]{2,1,0:T(8,128)}, u32[]{:S(2)}) copy-start(f32[4,128,256]{2,1,0:T(8,128)} %copy-done.6) | copy-start | bytes 1572868
  340.1 10.1 %copy-start.9 = (f32[4,128,256]{2,1,0:T(8,128)S(1)}, f32[4,128,256]{2,1,0:T(8,128)}, u32[]{:S(2)}) copy-start(f32[4,128,256]{2,1,0:T(8,128)} %copy-done.8) | copy-start | bytes 1572868
  341.9 27.3 %collective-permute-start.4 = (f32[4,128,256]{2,1,0:T(8,128)S(1)}, f32[4,128,256]{2,1,0:T(8,128)S(1)}, u32[]{:S(2)}, u32[]{:S(2)}) collective-permute-start(f32[4,128,256]{2,1,0:T(8,128)S(1)} %fusion.15), channel_id=1, source_target_pairs={{0,16},{16,0},{4,20},{20,4},{8,24},{24,8},{12,28},{28,12},{32,48},... | collective-permute-start | bytes 1572872 | tf_op jit(solution)/shard_map/ppermute | solution.py:30
  369.3 0.8 copy-start.10
  369.3 1.0 copy-start.12
  376.9 94.9 %copy-start.11 = (f32[4,128,256]{2,1,0:T(8,128)S(1)}, f32[4,128,256]{2,1,0:T(8,128)}, u32[]{:S(2)}) copy-start(f32[4,128,256]{2,1,0:T(8,128)} %copy-done.10) | copy-start | bytes 1572868
  376.9 94.9 %copy-start.13 = (f32[4,128,256]{2,1,0:T(8,128)S(1)}, f32[4,128,256]{2,1,0:T(8,128)}, u32[]{:S(2)}) copy-start(f32[4,128,256]{2,1,0:T(8,128)} %copy-done.12) | copy-start | bytes 1572868
Sparse Core Ops, SparseCore 0:
  10.1 33.8 all-gather.1
  83.3 34.9 reduce-scatter.1
where the time goes:
time: 482 us; the launch traced here: 481 us
  other arithmetic  276 us (57%)
  waiting for transfers between devices  112 us (23%)
  local copies, waits for them, and re-layouts  40.4 us (8%)
  matrix products  20.6 us (4%)
  starting transfers between devices  18.1 us (4%)
  between operations  14.5 us (3%)
    another operation x10, other arithmetic, merge_pair(): lower = jnp.linalg.cholesky(gram)  143 us
    another operation x7, other arithmetic, merge_pair(): jax.scipy.linalg.solve_triangular(factor, rhs, lower=True)  121 us
    all_gather x1, waiting for transfers between devices, local(): own_rows = lax.all_gather(samples, 'cols', axis=0, tiled=True)  36 us
    reduce_scatter x1, waiting for transfers between devices, local(): lax.psum_scatter(partial_value, 'cols', scatter_dimension=0, tiled=True)  34.4 us
    ppermute x3, waiting for transfers between devices, swapped(): return lax.ppermute(block, axis, route)  29.8 us
    gather x3, local copies, waits for them, and re-layouts, merge_pair(): picked = jax.vmap(lambda block, index: block[index])(stacked, chosen)  19.3 us
    gather x2, local copies, waits for them, and re-layouts, local(): picked = jnp.take(window, local_cols, axis=0)  11.1 us
    ppermute x3, starting transfers between devices, swapped(): return lax.ppermute(block, axis, route)  10.3 us
  transfers between devices with their start and end apart: 7, of which 7 were waited for; matrix products, arithmetic and copies ran while one was open for 2% of the time, Pallas kernels for 0%

commit v1 on v0

--- a/solution.py
+++ b/solution.py
@@ -5,6 +5,14 @@
 
 HIGHEST = lax.Precision.HIGHEST
 RIDGE = 0.25
+
+
+def tiled_gather(array, axis, dim):
+    size = lax.axis_size(axis)
+    repeats = [size if d == dim else 1 for d in range(array.ndim)]
+    return lax.all_to_all(
+        jnp.tile(array, repeats), axis, split_axis=dim, concat_axis=dim, tiled=True
+    )
 
 
 def padded(value, sides, width):
@@ -50,7 +58,7 @@
     cols_index = lax.axis_index("cols")
     clusters, slots, panels, _ = near_tiles.shape
     width = samples.shape[1]
-    own_rows = lax.all_gather(samples, "cols", axis=0, tiled=True)
+    own_rows = tiled_gather(samples, "cols", 0)
     near_rows = padded(own_rows, (("leaf", 0),), own_rows.shape[0])
     window = near_rows.reshape(3 * clusters, panels, width)
     local_cols = columns - (leaf_index - 1) * clusters

time: 482 us -> 468 us (0.971)
  waiting for transfers between devices: 112 us -> 73.8 us
  blocking collectives: 0 us -> 19.2 us
    all_gather x1 -> x0, waiting for transfers between devices: 36 us -> none  [local(): own_rows = lax.all_gather(samples, 'cols', axis=0, tiled=True)]
    all_to_all x0 -> x1, blocking collectives: none -> 19.2 us  [tiled_gather(): lax.all_to_all(jnp.tile(array, repeats), axis, split_axis=dim, concat_axi...]
  transfers between devices with their start and end apart: 7 -> 6, of which waited for: 7 -> 6; matrix products, arithmetic and copies ran while one was open for 2% -> 2% of each run, Pallas kernels for 0% -> 0%
where the time goes in v1:
time: 468 us; the launch traced here: 467 us
  other arithmetic  276 us (59%)
  waiting for transfers between devices  73.8 us (16%)
  local copies, waits for them, and re-layouts  41.7 us (9%)
  starting transfers between devices  21.3 us (5%)
  matrix products  20.6 us (4%)
  blocking collectives  19.2 us (4%)
  between operations  14.5 us (3%)
    another operation x10, other arithmetic, merge_pair(): lower = jnp.linalg.cholesky(gram)  143 us
    another operation x7, other arithmetic, merge_pair(): jax.scipy.linalg.solve_triangular(factor, rhs, lower=True)  121 us
    reduce_scatter x1, waiting for transfers between devices, local(): lax.psum_scatter(partial_value, 'cols', scatter_dimension=0, tiled=True)  33.4 us
    ppermute x3, waiting for transfers between devices, swapped(): return lax.ppermute(block, axis, route)  29.8 us
    gather x3, local copies, waits for them, and re-layouts, merge_pair(): picked = jax.vmap(lambda block, index: block[index])(stacked, chosen)  19.3 us
    all_to_all x1, blocking collectives, tiled_gather(): lax.all_to_all(jnp.tile(array, repeats), axis, split_axis=dim, concat_axi...  19.2 us
    gather x2, local copies, waits for them, and re-layouts, local(): picked = jnp.take(window, local_cols, axis=0)  11.1 us
    ppermute x3, starting transfers between devices, swapped(): return lax.ppermute(block, axis, route)  10.3 us
  transfers between devices with their start and end apart: 6, of which 6 were waited for; matrix products, arithmetic and copies ran while one was open for 2% of the time, Pallas kernels for 0%

profile of v1, /device:TPU:8, one launch (start us, length us, event | category | flops | bytes accessed | tf_op | source)
XLA Modules:
  0.0 466.9 jit_solution(1200284552215082906)
XLA Ops:
  8.4 19.2 %all_to_all.9 = bf16[4,512,256]{2,1,0:T(8,128)(2,1)S(1)} all-to-all(bf16[4,512,256]{2,1,0:T(8,128)(2,1)S(1)} %tile.2), channel_id=1, replica_groups=mesh['leaf'=128,'cols'=4] {'cols'}, dimensions={0} | all-to-all | bytes 2097152 | tf_op jit(solution)/shard_map/all_to_all | solution.py:13
  29.5 9.1 %collective-permute-start.1 = (bf16[2048,256]{1,0:T(8,128)(2,1)S(1)}, bf16[2048,256]{1,0:T(8,128)(2,1)}, u32[]{:S(2)}, u32[]{:S(2)}) collective-permute-start(bf16[2048,256]{1,0:T(8,128)(2,1)S(1)} %bitcast.78), channel_id=1, source_target_pairs={{4,0},{8,4},{12,8},{16,12},{20,16},{24,20},{28,24},{32,28},{36,32}... | collective-permute-start | bytes 3145736 | tf_op jit(solution)/shard_map/ppermute | solution.py:26
  40.3 8.9 %collective-permute-done = bf16[2048,256]{1,0:T(8,128)(2,1)} collective-permute-done((bf16[2048,256]{1,0:T(8,128)(2,1)S(1)}, bf16[2048,256]{1,0:T(8,128)(2,1)}, u32[]{:S(2)}, u32[]{:S(2)}) %collective-permute-start) | collective-permute-done | bytes 1048608 | tf_op jit(solution)/shard_map/ppermute | solution.py:25
  50.9 3.0 pad_maximum_fusion
  53.9 4.6 gather_fusion
  58.5 6.4 %copy.40 = bf16[16,4,128,256]{2,3,1,0:T(8,128)(2,1)} copy(bf16[16,4,128,256]{3,2,1,0:T(8,128)(2,1)} %bitcast.70) | data formatting | bytes 8388608 | tf_op jit(solution)/shard_map/jit(_take)/gather | solution.py:65
  64.9 4.8 %fusion.6 = f32[16,128,256]{1,2,0:T(8,128)} fusion(bf16[16,4,128,128]{3,2,1,0:T(8,128)(2,1)S(1)} %copy-done, bf16[16,4,128,256]{2,3,1,0:T(8,128)(2,1)} %copy.40, pred[16,4]{1,0:T(8,128)(4,1)S(1)} %copy.38, bf16[16,4]{1,0:T(8,128)(2,1)S(1)} %compare_convert_fusion), kind=kOutput, calls=%fused_computation.11 | convolution fusion | flops 541065216 | bytes 8388800 | tf_op jit(solution)/shard_map/ksij,ksjn->kin/dot_general | solution.py:69
  70.6 33.4 %reduce-scatter.2.cloned.1.call-done = f32[4,128,256]{1,2,0:T(8,128)} async-done(((f32[16,128,256]{1,2,0:T(8,128)}), f32[4,128,256]{1,2,0:T(8,128)}) %reduce-scatter.2.cloned.1.call-update) | async-done | bytes 524304 | tf_op jit(solution)/shard_map/reduce_scatter | solution.py:72
  112.8 6.4 %gather_fusion.1 = f32[512,256]{1,0:T(8,128)} fusion(f32[4,256,256]{2,1,0:T(8,128)S(1)} %copy.41, s32[512]{0:T(512)S(1)} %get-tuple-element.14), kind=kCustom, calls=%fused_computation.1 | custom fusion | bytes 1052672 | tf_op jit(solution)/shard_map/vmap()/gather | solution.py:43
  121.1 46.9 %custom-call.16 = f32[4,128,128]{2,1,0:T(8,128)S(1)} custom-call(f32[4,128,128]{2,1,0:T(8,128)S(1)} %fusion.20), custom_call_target="Cholesky" | custom-call | tf_op jit(solution)/shard_map/jit(cholesky)/cholesky | solution.py:48
  168.3 39.3 %custom-call.17 = f32[4,1,128,128]{2,3,1,0:T(8,128)S(1)} custom-call(f32[4,1,128,128]{3,2,1,0:T(8,128)S(1)} %select_bitcast_fusion.2), custom_call_target="InvertDiagBlocksLowerTriangular" | custom-call | tf_op jit(solution)/shard_map/vmap(jit(_solve_triangular))/triangular_solve | solution.py:50
  209.3 3.8 collective-permute-start.3
  213.9 11.3 %collective-permute-done.3 = f32[4,128,256]{2,1,0:T(8,128)S(1)} collective-permute-done((f32[4,128,256]{2,1,0:T(8,128)S(1)}, f32[4,128,256]{2,1,0:T(8,128)S(1)}, u32[]{:S(2)}, u32[]{:S(2)}) %collective-permute-start.3) | collective-permute-done | bytes 524320 | tf_op jit(solution)/shard_map/ppermute | solution.py:38
  226.3 6.4 %gather_fusion.2 = f32[512,256]{1,0:T(8,128)} fusion(f32[4,256,256]{2,1,0:T(8,128)S(1)} %pad_maximum_fusion.2, s32[512]{0:T(512)S(1)} %get-tuple-element.15), kind=kCustom, calls=%fused_computation.2 | custom fusion | bytes 1052672 | tf_op jit(solution)/shard_map/vmap()/gather | solution.py:43
  232.6 1.9 fusion.10
  237.1 47.7 %custom-call.18 = f32[4,128,128]{2,1,0:T(8,128)S(1)} custom-call(f32[4,128,128]{2,1,0:T(8,128)} %fusion.17), custom_call_target="Cholesky" | custom-call | tf_op jit(solution)/shard_map/jit(cholesky)/cholesky | solution.py:48
  285.8 40.1 %custom-call.19 = f32[4,1,128,128]{2,3,1,0:T(8,128)S(1)} custom-call(f32[4,1,128,128]{3,2,1,0:T(8,128)} %select_bitcast_fusion.1), custom_call_target="InvertDiagBlocksLowerTriangular" | custom-call | tf_op jit(solution)/shard_map/vmap(jit(_solve_triangular))/triangular_solve | solution.py:50
  327.7 4.6 collective-permute-start.4
  332.4 2.9 convolution_multiply_fusion
  337.8 17.2 %collective-permute-done.4 = f32[4,128,256]{2,1,0:T(8,128)S(1)} collective-permute-done((f32[4,128,256]{2,1,0:T(8,128)S(1)}, f32[4,128,256]{2,1,0:T(8,128)S(1)}, u32[]{:S(2)}, u32[]{:S(2)}) %collective-permute-start.4) | collective-permute-done | bytes 524320 | tf_op jit(solution)/shard_map/ppermute | solution.py:38
  356.1 6.6 %gather_fusion.3 = f32[512,256]{1,0:T(8,128)} fusion(f32[4,256,256]{2,1,0:T(8,128)S(1)} %pad_maximum_fusion.3, s32[512]{0:T(512)S(1)} %fusion.35), kind=kCustom, calls=%fused_computation.3 | custom fusion | bytes 1052672 | tf_op jit(solution)/shard_map/vmap()/gather | solution.py:43
  362.7 1.9 fusion.11
  367.1 47.7 %custom-call.20 = f32[4,128,128]{2,1,0:T(8,128)S(1)} custom-call(f32[4,128,128]{2,1,0:T(8,128)} %fusion.14), custom_call_target="Cholesky" | custom-call | tf_op jit(solution)/shard_map/jit(cholesky)/cholesky | solution.py:48
  415.8 40.1 %custom-call.21 = f32[4,1,128,128]{2,3,1,0:T(8,128)S(1)} custom-call(f32[4,1,128,128]{3,2,1,0:T(8,128)} %select_bitcast_fusion), custom_call_target="InvertDiagBlocksLowerTriangular" | custom-call | tf_op jit(solution)/shard_map/vmap(jit(_solve_triangular))/triangular_solve | solution.py:50
  (82 shorter events, 38.0 us)
Async XLA Ops:
  7.2 57.8 %copy-start = (bf16[16,4,128,128]{3,2,1,0:T(8,128)(2,1)S(1)}, bf16[16,4,128,128]{3,2,1,0:T(8,128)(2,1)}, u32[]{:S(2)}) copy-start(bf16[16,4,128,128]{3,2,1,0:T(8,128)(2,1)} %param.11) | copy-start | bytes 6291460
  7.2 96.8 %reduce-scatter.2.cloned.1.call-start = ((), (), s32[]{:S(2)}) async-start(), calls=%async_computation.2 | async-start | bytes 2621440 | tf_op jit(solution)/shard_map/reduce_scatter | solution.py:72
  27.6 21.7 %collective-permute-start = (bf16[2048,256]{1,0:T(8,128)(2,1)S(1)}, bf16[2048,256]{1,0:T(8,128)(2,1)}, u32[]{:S(2)}, u32[]{:S(2)}) collective-permute-start(bf16[2048,256]{1,0:T(8,128)(2,1)S(1)} %bitcast.77), channel_id=1, source_target_pairs={{0,4},{4,8},{8,12},{12,16},{16,20},{20,24},{24,28},{28,32},{32,36}... | collective-permute-start | bytes 3145736 | tf_op jit(solution)/shard_map/ppermute | solution.py:25
  29.5 21.4 %collective-permute-start.1 = (bf16[2048,256]{1,0:T(8,128)(2,1)S(1)}, bf16[2048,256]{1,0:T(8,128)(2,1)}, u32[]{:S(2)}, u32[]{:S(2)}) collective-permute-start(bf16[2048,256]{1,0:T(8,128)(2,1)S(1)} %bitcast.78), channel_id=1, source_target_pairs={{4,0},{8,4},{12,8},{16,12},{20,16},{24,20},{28,24},{32,28},{36,32}... | collective-permute-start | bytes 3145736 | tf_op jit(solution)/shard_map/ppermute | solution.py:26
  104.0 4.0 collective-permute-start.2
  109.1 0.8 copy-start.3
  109.1 1.0 copy-start.5
  209.3 16.0 %copy-start.1 = (f32[4,128,256]{2,1,0:T(8,128)}, f32[4,128,256]{2,1,0:T(8,128)S(1)}, u32[]{:S(2)}) copy-start(f32[4,128,256]{2,1,0:T(8,128)S(1)} %fusion.18) | copy-start | bytes 1572868
  209.3 15.9 %collective-permute-start.3 = (f32[4,128,256]{2,1,0:T(8,128)S(1)}, f32[4,128,256]{2,1,0:T(8,128)S(1)}, u32[]{:S(2)}, u32[]{:S(2)}) collective-permute-start(f32[4,128,256]{2,1,0:T(8,128)S(1)} %fusion.18), channel_id=1, source_target_pairs={{0,8},{8,0},{4,12},{12,4},{16,24},{24,16},{20,28},{28,20},{32,40},... | collective-permute-start | bytes 1572872 | tf_op jit(solution)/shard_map/ppermute | solution.py:38
  225.3 0.8 copy-start.6
  225.3 1.0 copy-start.8
  232.6 99.7 %copy-start.2 = (f32[4,128,256]{2,1,0:T(8,128)S(1)}, f32[4,128,256]{2,1,0:T(8,128)}, u32[]{:S(2)}) copy-start(f32[4,128,256]{2,1,0:T(8,128)} %copy-done.1) | copy-start | bytes 1572868
  232.6 99.7 %copy-start.4 = (f32[4,128,256]{1,2,0:T(8,128)S(1)}, f32[4,128,256]{1,2,0:T(8,128)}, u32[]{:S(2)}) copy-start(f32[4,128,256]{1,2,0:T(8,128)} %copy-done.3) | copy-start | bytes 1572868
  325.9 10.1 %copy-start.7 = (f32[4,128,256]{2,1,0:T(8,128)S(1)}, f32[4,128,256]{2,1,0:T(8,128)}, u32[]{:S(2)}) copy-start(f32[4,128,256]{2,1,0:T(8,128)} %copy-done.6) | copy-start | bytes 1572868
  325.9 10.1 %copy-start.9 = (f32[4,128,256]{2,1,0:T(8,128)S(1)}, f32[4,128,256]{2,1,0:T(8,128)}, u32[]{:S(2)}) copy-start(f32[4,128,256]{2,1,0:T(8,128)} %copy-done.8) | copy-start | bytes 1572868
  327.7 27.3 %collective-permute-start.4 = (f32[4,128,256]{2,1,0:T(8,128)S(1)}, f32[4,128,256]{2,1,0:T(8,128)S(1)}, u32[]{:S(2)}, u32[]{:S(2)}) collective-permute-start(f32[4,128,256]{2,1,0:T(8,128)S(1)} %fusion.15), channel_id=1, source_target_pairs={{0,16},{16,0},{4,20},{20,4},{8,24},{24,8},{12,28},{28,12},{32,48},... | collective-permute-start | bytes 1572872 | tf_op jit(solution)/shard_map/ppermute | solution.py:38
  355.1 0.8 copy-start.10
  355.1 1.0 copy-start.12
  362.7 94.9 %copy-start.11 = (f32[4,128,256]{2,1,0:T(8,128)S(1)}, f32[4,128,256]{2,1,0:T(8,128)}, u32[]{:S(2)}) copy-start(f32[4,128,256]{2,1,0:T(8,128)} %copy-done.10) | copy-start | bytes 1572868
  362.7 94.9 %copy-start.13 = (f32[4,128,256]{2,1,0:T(8,128)S(1)}, f32[4,128,256]{2,1,0:T(8,128)}, u32[]{:S(2)}) copy-start(f32[4,128,256]{2,1,0:T(8,128)} %copy-done.12) | copy-start | bytes 1572868
Sparse Core Ops, SparseCore 0:
  69.9 34.0 reduce-scatter.1
